TPU v7x, 256 devices: a whole 4x4x8 slice. The times are simulated.
256 devices in a mesh: seq: 32 (over y_lo, z, core), head: 8 (over y_hi, x).
Axes of the slice: x: 4, y: 4 (y_hi: 2, y_lo: 2; y = y_hi * 2 + y_lo), z: 8, core: 2. Of those that a mesh axis runs over, the one named last changes fastest.
Arguments:
- teacher: bfloat16 [1, 8192, 4096], P(None, 'seq', 'head'), may hold values from -32 to 32
- student: bfloat16 [1, 8192, 1792], P(None, 'seq', 'head'), may hold values from -32 to 32
- weights: float32 [8192], P('seq'), may hold values from 1 to 32
Outputs:
- mean_loss: float32 [], replicated
- student_grad: float32 [1, 8192, 1792], P(None, 'seq', 'head')
All inputs are finite; a program needn't handle non-finite values.
Results may differ from a plain program's by a relative error of at most 0.0011.
Values may be sent and summed in bfloat16 or wider, within the bound.
No kernel may reach another device: no remote copies, remote signals or barrier semaphores. Data moves between devices by JAX's collectives and lax.ppermute only.
A program may use at most 128 MiB of HBM per device.

v0:
```python
import functools
import math

import jax
import jax.numpy as jnp
from jax import lax
from jax.experimental import pallas as pl
from jax.experimental.pallas import tpu as pltpu
from jax.sharding import Mesh
from jax.sharding import PartitionSpec as P

TW = 256
SW = 112
HEADS = 16
SEQ = ("yl", "z", "c")
HEAD = ("yh", "x")
LOG2E = math.log2(math.e)
CT = LOG2E / math.sqrt(TW)
CS = LOG2E / math.sqrt(SW)
TOK = 256
PACK = 384
F32 = jnp.float32
BF16 = jnp.bfloat16
NT = (((1,), (1,)), ((), ()))
PARAMS = pltpu.CompilerParams(vmem_limit_bytes=20 * 1024 * 1024)


def whole(n):
    return [pl.BlockSpec(memory_space=pltpu.VMEM)] * n


HBM = pl.BlockSpec(memory_space=pltpu.HBM)
SCALAR = pl.BlockSpec(memory_space=pltpu.SMEM)
TEACH, STUD = slice(0, TW), slice(TW, PACK)


def in_hbm(array):
    return pltpu.with_memory_space_constraint(array, pltpu.HBM)


def nt_dot(a, b):
    return lax.dot_general(a, b, NT, preferred_element_type=F32)


def prep_kernel(yl_ref, teach_in, stud_in, weight_in, own_ref, give_ref, teach_ref, stud_ref, weight_ref, sems):
    copies = [
        pltpu.make_async_copy(source, target, sems.at[i])
        for i, (source, target) in enumerate(
            ((teach_in, teach_ref), (stud_in, stud_ref), (weight_in, weight_ref))
        )
    ]
    for copy in copies:
        copy.start()
    for copy in copies:
        copy.wait()
    yl = yl_ref[0]
    weight = weight_ref[...]
    high = weight.astype(BF16).astype(F32)
    middle = (weight - high).astype(BF16).astype(F32)
    low = weight - high - middle
    row = lax.broadcasted_iota(jnp.int32, (16, TOK), 0)
    extra = jnp.where(row == 0, high, jnp.where(row == 1, middle, jnp.where(row == 2, low, 0.0)))
    packs = []
    for h in range(2):
        stud = stud_ref[h * SW : (h + 1) * SW, :].astype(F32)
        packs.append(jnp.concatenate([stud, extra], axis=0))
    first = yl == 0
    for ref, flip in ((own_ref, first), (give_ref, jnp.logical_not(first))):
        ref[:, TW:] = jnp.where(flip, packs[0], packs[1]).T.astype(BF16)
        ref[:, :TW] = jnp.where(flip, teach_ref[:, :TW].astype(F32), teach_ref[:, TW:].astype(F32)).astype(BF16)


def prepare(yl, teacher, stud_t, weights):
    packet = jax.ShapeDtypeStruct((TOK, PACK), BF16)
    return pl.pallas_call(
        prep_kernel,
        out_shape=(packet, packet),
        in_specs=[SCALAR] + [HBM] * 3,
        out_specs=tuple(whole(2)),
        scratch_shapes=[
            pltpu.VMEM((TOK, 2 * TW), BF16),
            pltpu.VMEM((2 * SW, TOK), BF16),
            pltpu.VMEM((1, TOK), F32),
            pltpu.SemaphoreType.DMA((3,)),
        ],
        compiler_params=PARAMS,
        name="prepare",
    )(yl, in_hbm(teacher), in_hbm(stud_t), in_hbm(weights))


def pair_kernel(own, sib, out):
    out[:TOK, :] = own[...]
    out[TOK:, :] = sib[...]


def pair_up(own, sib):
    return pl.pallas_call(
        pair_kernel,
        out_shape=jax.ShapeDtypeStruct((2 * TOK, PACK), BF16),
        in_specs=whole(2),
        out_specs=whole(1)[0],
        compiler_params=PARAMS,
        name="pair_up",
    )(own, sib)


def open_packets(pairs, held, weight_ref):
    lane = lax.broadcasted_iota(jnp.int32, (2 * TOK, PACK - TW), 1)
    for i, pair in enumerate(pairs):
        at = slice(2 * i * TOK, 2 * (i + 1) * TOK)
        held[at, :TW] = pair[:, :TW]
        stud = pair[:, TW:].astype(F32)
        held[at, TW:] = jnp.where(lane < SW, stud, 0.0).astype(BF16)
        columns = stud.T
        weight = columns[SW : SW + 1] + columns[SW + 1 : SW + 2] + columns[SW + 2 : SW + 3]
        weight_ref[0:1, at] = weight
        weight_ref[1:2, at] = jnp.log(weight) * LOG2E


def take_stats(held, key, before, out, last):
    for i in range(2):
        at = slice(2 * i * TOK, 2 * (i + 1) * TOK)
        t = nt_dot(key[:, TEACH], held[at, TEACH]).reshape(-1, 8, 2 * TOK) * CT
        s = nt_dot(key[:, STUD], held[at, STUD]).reshape(-1, 8, 2 * TOK) * CS
        t_max, s_max = jnp.max(t, axis=0), jnp.max(s, axis=0)
        if before is not None:
            state = [before[8 * k : 8 * k + 8, at] for k in range(5)]
            t_max, s_max = jnp.maximum(t_max, state[0]), jnp.maximum(s_max, state[3])
        t_exp = jnp.exp2(t - t_max[None])
        s_exp = jnp.exp2(s - s_max[None])
        t_sum, s_sum = jnp.sum(t_exp, axis=0), jnp.sum(s_exp, axis=0)
        cross = jnp.sum(t_exp * (t - s), axis=0)
        if before is not None:
            t_keep, s_keep = jnp.exp2(state[0] - t_max), jnp.exp2(state[3] - s_max)
            t_sum = t_sum + state[1] * t_keep
            cross = cross + state[2] * t_keep
            s_sum = s_sum + state[4] * s_keep
        if last:
            t_top = jnp.max(t_max, axis=0, keepdims=True)
            s_top = jnp.max(s_max, axis=0, keepdims=True)
            t_keep, s_keep = jnp.exp2(t_max - t_top), jnp.exp2(s_max - s_top)
            out[0:1, at] = t_top
            out[1:2, at] = jnp.sum(t_sum * t_keep, axis=0, keepdims=True)
            out[2:3, at] = jnp.sum(cross * t_keep, axis=0, keepdims=True)
            out[3:4, at] = s_top
            out[4:5, at] = jnp.sum(s_sum * s_keep, axis=0, keepdims=True)
        else:
            for k, value in enumerate((t_max, t_sum, cross, s_max, s_sum)):
                out[8 * k : 8 * k + 8, at] = value


def own_keys(held, columns):
    return jnp.concatenate([held[:TOK, columns], held[2 * TOK : 3 * TOK, columns]], axis=0)


def first_kernel(own_ref, got_ref, state, held, weight_ref):
    open_packets((own_ref, got_ref), held, weight_ref)
    take_stats(held, own_keys(held, slice(None)), None, state, False)


def more_kernel(last, held, key, before, out):
    take_stats(held, key, before, out, last)


def stat_cost(pairs):
    return pl.CostEstimate(flops=2 * pairs * 512, bytes_accessed=pairs * 4, transcendentals=2 * pairs)


def first_stats(own_pair, got_pair):
    return pl.pallas_call(
        first_kernel,
        out_shape=(
            jax.ShapeDtypeStruct((40, 4 * TOK), F32),
            jax.ShapeDtypeStruct((4 * TOK, PACK), BF16),
            jax.ShapeDtypeStruct((8, 4 * TOK), F32),
        ),
        in_specs=whole(2),
        out_specs=tuple(whole(3)),
        compiler_params=PARAMS,
        cost_estimate=stat_cost(4 * TOK * 2 * TOK),
        name="first_stats",
    )(own_pair, got_pair)


def more_stats(held, key, before, last=False):
    pairs = 4 * TOK * key.shape[0]
    return pl.pallas_call(
        functools.partial(more_kernel, last),
        out_shape=jax.ShapeDtypeStruct((8 if last else 40, 4 * TOK), F32),
        in_specs=whole(3),
        out_specs=whole(1)[0],
        input_output_aliases={} if last else {2: 0},
        compiler_params=PARAMS,
        cost_estimate=stat_cost(pairs),
        name="more_stats",
    )(held, key, before)


def merge_kernel(mine, sib, weight_ref, norm_ref, send_ref):
    total = jnp.zeros((1, TOK), F32)
    for i in range(4):
        at = slice(i * TOK, (i + 1) * TOK)
        there = slice((i ^ 1) * TOK, ((i ^ 1) + 1) * TOK)
        a = [mine[k : k + 1, at] for k in range(5)]
        b = [sib[k : k + 1, there] for k in range(5)]
        t_max, s_max = jnp.maximum(a[0], b[0]), jnp.maximum(a[3], b[3])
        ta, tb = jnp.exp2(a[0] - t_max), jnp.exp2(b[0] - t_max)
        sa, sb = jnp.exp2(a[3] - s_max), jnp.exp2(b[3] - s_max)
        t_sum, s_sum = a[1] * ta + b[1] * tb, a[4] * sa + b[4] * sb
        cross = a[2] * ta + b[2] * tb
        t_norm = t_max + jnp.log(t_sum) * LOG2E
        s_norm = s_max + jnp.log(s_sum) * LOG2E
        total = total + weight_ref[0:1, at] * (cross / t_sum - t_norm + s_norm)
        t_norm, s_norm = t_norm - weight_ref[1:2, at], s_norm - weight_ref[1:2, at]
        norm_ref[0:1, at] = t_norm
        norm_ref[1:2, at] = s_norm
        for z in range(8):
            send_ref[z, 0:1, at] = t_norm
            send_ref[z, 1:2, at] = s_norm
    loss = jnp.broadcast_to(jnp.sum(total, axis=1, keepdims=True), (2, 128))
    for z in range(8):
        send_ref[z, :, 4 * TOK :] = loss


def merge(mine, sib, weight):
    return pl.pallas_call(
        merge_kernel,
        out_shape=(jax.ShapeDtypeStruct((8, 4 * TOK), F32), jax.ShapeDtypeStruct((8, 2, 4 * TOK + 128), F32)),
        in_specs=whole(3),
        out_specs=tuple(whole(2)),
        compiler_params=PARAMS,
        name="merge",
    )(mine, sib, weight)


def column_of(row):
    return jnp.broadcast_to(row, (128, 128)).T


def slopes_of(t, s, t_norm, s_norm):
    return jnp.exp2(s - s_norm) - jnp.exp2(t - t_norm)


class Keys:
    def __init__(self, held, refs, late, sems):
        self.held, self.near, self.opposite, self.far, self.late = held, refs[:4], refs[4:6], refs[6:8], late
        self.copies = [pltpu.make_async_copy(self.far[i], late.at[i], sems.at[i]) for i in range(2)]

    def start(self):
        for copy in self.copies:
            copy.start()

    def wait(self):
        for copy in self.copies:
            copy.wait()

    def block(self, slot, columns):
        if slot == 0:
            return own_keys(self.held, columns)
        if slot <= 4:
            return self.near[slot - 1][:, columns]
        if slot == 5:
            return jnp.concatenate([self.opposite[0][:, columns], self.opposite[1][:, columns]], axis=0)
        return self.late[slot - 6, :, columns]

    def piece(self, i, columns):
        if i < 4:
            return self.near[i][:, columns]
        if i < 6:
            return self.held[(i - 4) * 2 * TOK : (i - 4) * 2 * TOK + TOK, columns]
        if i < 8:
            return self.opposite[i - 6][:, columns]
        return self.late[i - 8, :, columns]


STEPS = (0, 2, 2, 3, 3, 4, 1, 1)
KEY_SPECS = whole(6) + [HBM] * 2
KEY_SCRATCH = [pltpu.VMEM((2, 2 * TOK, PACK), BF16), pltpu.SemaphoreType.DMA((4,))]


def as_operands(packets):
    return [*packets[:6], *(in_hbm(p) for p in packets[6:])]


def row_kernel(held, norm_ref, *refs):
    result, t_norm, s_norm, out, late, sems = refs[8:]
    keys = Keys(held, refs[:8], late, sems)
    keys.start()
    for b in range(8):
        at = slice(b * 128, (b + 1) * 128)
        t_norm[at, :] = column_of(norm_ref[0:1, at])
        s_norm[at, :] = column_of(norm_ref[1:2, at])

    def step(half, carry):
        at = pl.ds(pl.multiple_of(half * 2 * TOK, 2 * TOK), 2 * TOK)
        tn, sn = t_norm[at, :], s_norm[at, :]
        for i in range(10):
            if i == 8:
                pl.when(half == 0)(keys.wait)
            stud = keys.piece(i, STUD)
            t = nt_dot(held[at, TEACH], keys.piece(i, TEACH)) * CT
            s = nt_dot(held[at, STUD], stud) * CS
            p = jnp.concatenate(
                [slopes_of(t[:, k : k + 128], s[:, k : k + 128], tn, sn) for k in range(0, s.shape[1], 128)], axis=1
            )
            part = jnp.dot(p.astype(BF16), stud, preferred_element_type=F32)
            out[at, :] = part if i == 0 else out[at, :] + part
        pltpu.make_async_copy(out.at[at, :], result.at[at, :], sems.at[2 + half]).start()
        return carry

    lax.fori_loop(0, 2, step, 0)
    for half in range(2):
        at = slice(half * 2 * TOK, (half + 1) * 2 * TOK)
        pltpu.make_async_copy(out.at[at, :], result.at[at, :], sems.at[2 + half]).wait()


def row_part(held, norms, packets):
    pairs = 4 * TOK * 4096
    return pl.pallas_call(
        row_kernel,
        out_shape=pltpu.HBM((4 * TOK, 128), F32),
        in_specs=whole(2) + KEY_SPECS,
        out_specs=HBM,
        scratch_shapes=[pltpu.VMEM((4 * TOK, 128), F32)] * 3 + KEY_SCRATCH,
        compiler_params=PARAMS,
        cost_estimate=pl.CostEstimate(flops=2 * pairs * 640, bytes_accessed=pairs * 4, transcendentals=2 * pairs),
        name="row_part",
    )(held, norms, *as_operands(packets))


def col_kernel(query_at, place_ref, held, stat_ref, *refs):
    row_ref, keep, give = refs[8:11]
    acc, rows, late, sems = refs[-4:]
    if len(refs) == 16:
        total = jnp.sum(stat_ref[:, 0, 4 * TOK :], axis=0, keepdims=True)
        refs[11][...] = jnp.broadcast_to(total[None], (16, 1, 128))
    keys = Keys(held, refs[:8], late, sems)
    keys.start()
    at = slice(query_at, query_at + 2 * TOK)
    copy = pltpu.make_async_copy(row_ref.at[at, :], rows, sems.at[2])
    copy.start()
    toward = jnp.where(place_ref[0] == 0, 7, 1)
    for slot in range(8):
        if slot == 6:
            keys.wait()
            copy.wait()
        source = lax.rem(place_ref[1] + toward * STEPS[slot], 8)
        if slot in (0, 5):
            t_norm, s_norm = (
                jnp.concatenate([stat_ref[source, i : i + 1, k : k + TOK] for k in (0, 2 * TOK)], axis=1)
                for i in range(2)
            )
        else:
            plane = 2 * TOK * (1 - slot % 2 if slot < 5 else slot % 2)
            t_norm, s_norm = (stat_ref[source, i : i + 1, plane : plane + 2 * TOK] for i in range(2))
        stud = keys.block(slot, STUD)
        t = nt_dot(held[at, TEACH], keys.block(slot, TEACH)) * CT
        s = nt_dot(held[at, STUD], stud) * CS
        p = slopes_of(t, s, t_norm, s_norm).astype(BF16)
        part = jnp.dot(p, stud, preferred_element_type=F32)
        acc[...] = part if slot == 0 else acc[...] + part
    for i, out in enumerate((keep, give)):
        part = slice(i * TOK, (i + 1) * TOK)
        out[...] = (acc[part, :] + rows[part, :]).T[:SW, :] * (1.0 / math.sqrt(SW))


def col_part(place, held, stats, packets, rows, query_at, with_loss):
    pairs = 2 * TOK * 4096
    part = jax.ShapeDtypeStruct((SW, TOK), F32)
    return pl.pallas_call(
        functools.partial(col_kernel, query_at),
        out_shape=(part, part) + with_loss * (jax.ShapeDtypeStruct((16, 1, 128), F32),),
        in_specs=[SCALAR] + whole(2) + KEY_SPECS + [HBM],
        out_specs=tuple(whole(2 + with_loss)),
        scratch_shapes=[pltpu.VMEM((2 * TOK, 128), F32)] * 2 + KEY_SCRATCH,
        compiler_params=PARAMS,
        cost_estimate=pl.CostEstimate(flops=2 * pairs * 640, bytes_accessed=pairs * 4, transcendentals=2 * pairs),
        name="col_part",
    )(place, held, stats, *as_operands(packets), in_hbm(rows))


def onward(array):
    pairs = [(2 * z + c, 2 * ((z + (-1) ** c) % 8) + c) for z in range(8) for c in range(2)]
    return lax.ppermute(array, ("z", "c"), pairs)


def tied(*arrays):
    return lax.optimization_barrier(arrays)


def swap(array, axis):
    n = 4 if isinstance(axis, tuple) else 2
    return lax.ppermute(array, axis, [(i, n - 1 - i) for i in range(n)])


def local(teacher, student, weights):
    yl, z, c = lax.axis_index("yl"), lax.axis_index("z"), lax.axis_index("c")
    own, give = prepare(yl.reshape(1), teacher[0], student[0].T, weights.reshape(1, TOK))
    got = swap(give, "yl")
    own_pair = pair_up(own, swap(own, "c"))
    a1 = onward(own_pair)
    got_pair = pair_up(got, swap(got, "c"))
    a1, sent_pair = tied(a1, got_pair)
    b1 = onward(sent_pair)
    a2 = onward(a1)
    state, held, weight = first_stats(own_pair, got_pair)
    b1, state = tied(b1, state)
    b2 = onward(b1)
    state = more_stats(held, a1, state)
    a2, state = tied(a2, state)
    a3 = onward(a2)
    state = more_stats(held, b1, state)
    b2, state = tied(b2, state)
    b3 = onward(b2)
    state = more_stats(held, a2, state)
    a3, state = tied(a3, state)
    a4 = onward(a3[:TOK])
    state = more_stats(held, b2, state)
    b3, state = tied(b3, state)
    b4 = onward(b3[:TOK])
    for packets in (a3, b3, a4):
        state = more_stats(held, packets, state)
    state = more_stats(held, b4, state, last=True)
    packets = (a2, b2, a3, b3, a4, b4, a1, b1)
    norms, send = merge(state, swap(state, "c"), weight)
    stats = lax.all_to_all(send, "z", 0, 0, tiled=True)
    rows = row_part(held, norms, packets)
    place = jnp.stack([c, z])
    far_keep, far_give, loss = col_part(place, held, stats, packets, rows, 2 * TOK, True)
    losses = lax.all_to_all(loss, ("yl", *HEAD), 0, 0, tiled=True)
    other = swap(far_keep, "yl") + swap(far_give, ("yl", "c"))
    rows, other = tied(rows, other)
    near_keep, near_give = col_part(place, held, stats, packets, rows, 0, False)
    mine = near_keep + swap(near_give, "c")
    grad = jnp.where(yl == 0, jnp.concatenate([mine, other]), jnp.concatenate([other, mine]))
    mean_loss = jnp.sum(losses[:, 0, 0]) * (math.log(2.0) / (HEADS * 8192))
    return mean_loss, grad.T[None]


def solution(mesh):
    finer = Mesh(mesh.devices.reshape(2, 8, 2, 2, 4), ("yl", "z", "c", "yh", "x"))
    return jax.shard_map(
        local,
        mesh=finer,
        in_specs=(P(None, SEQ, HEAD), P(None, SEQ, HEAD), P(SEQ)),
        out_specs=(P(), P(None, SEQ, HEAD)),
        check_vma=False,
    )
```

profile of v0, /device:TPU:1, one launch (start us, length us, event | category | flops | bytes accessed | tf_op | source)
XLA Modules:
  0.0 91.6 jit_solution(17511830721408486445)
XLA Ops:
  0.6 1.2 %prepare.1 = (bf16[256,384]{1,0:T(8,128)(2,1)S(1)}, bf16[256,384]{1,0:T(8,128)(2,1)S(1)}) custom-call(s32[1]{0:T(128)} %bitcast.2.yl_ref, bf16[256,512]{1,0:T(8,128)(2,1)} %bitcast.12, bf16[224,256]{1,0:T(8,128)(2,1)} %bitcast.13, f32[1,256]{1,0:T(1,128)} %bitcast.14), custom_call_target="tpu_custom_call" | custom-call | tf_op jit(solution)/shard_map/prepare/pallas_call | solution.py:75
  1.8 3.3 %collective-permute-start = (bf16[256,384]{1,0:T(8,128)(2,1)S(1)}, bf16[256,384]{1,0:T(8,128)(2,1)S(1)}, u32[]{:S(2)}, u32[]{:S(2)}) collective-permute-start(bf16[256,384]{1,0:T(8,128)(2,1)S(1)} %get-tuple-element.28.own), channel_id=1, source_target_pairs={{0,8},{8,0},{1,9},{9,1},{2,10},{10,2},{3,11},{11,3},{4,12},{12,4},... | collective-permute-start | bytes 589832 | tf_op jit(solution)/shard_map/ppermute | solution.py:393
  5.2 0.0 collective-permute-start.1
  5.2 1.1 %collective-permute-done.sib = bf16[256,384]{1,0:T(8,128)(2,1)S(1)} collective-permute-done((bf16[256,384]{1,0:T(8,128)(2,1)S(1)}, bf16[256,384]{1,0:T(8,128)(2,1)S(1)}, u32[]{:S(2)}, u32[]{:S(2)}) %collective-permute-start) | collective-permute-done | bytes 196640 | tf_op jit(solution)/shard_map/ppermute | solution.py:393
  6.3 4.2 %collective-permute-start.3 = (bf16[512,384]{1,0:T(8,128)(2,1)S(1)}, bf16[512,384]{1,0:T(8,128)(2,1)S(1)}, u32[]{:S(2)}, u32[]{:S(2)}) collective-permute-start(bf16[512,384]{1,0:T(8,128)(2,1)S(1)} %pair_up.2.own_ref), channel_id=1, source_target_pairs={{0,16},{8,120},{16,32},{24,8},{32,48},{40,24},{48,64},{56,40},{64,... | collective-permute-start | bytes 1179656 | tf_op jit(solution)/shard_map/ppermute | solution.py:384
  10.4 1.2 %collective-permute-done.1.own = bf16[256,384]{1,0:T(8,128)(2,1)S(1)} collective-permute-done((bf16[256,384]{1,0:T(8,128)(2,1)S(1)}, bf16[256,384]{1,0:T(8,128)(2,1)S(1)}, u32[]{:S(2)}, u32[]{:S(2)}) %collective-permute-start.1) | collective-permute-done | bytes 196640 | tf_op jit(solution)/shard_map/ppermute | solution.py:393
  11.6 0.9 collective-permute-start.2
  12.5 1.1 %collective-permute-done.2.sib = bf16[256,384]{1,0:T(8,128)(2,1)S(1)} collective-permute-done((bf16[256,384]{1,0:T(8,128)(2,1)S(1)}, bf16[256,384]{1,0:T(8,128)(2,1)S(1)}, u32[]{:S(2)}, u32[]{:S(2)}) %collective-permute-start.2) | collective-permute-done | bytes 196640 | tf_op jit(solution)/shard_map/ppermute | solution.py:393
  13.6 1.6 %collective-permute-done.3.key.refs_6_ = bf16[512,384]{1,0:T(8,128)(2,1)S(1)} collective-permute-done((bf16[512,384]{1,0:T(8,128)(2,1)S(1)}, bf16[512,384]{1,0:T(8,128)(2,1)S(1)}, u32[]{:S(2)}, u32[]{:S(2)}) %collective-permute-start.3) | collective-permute-done | bytes 393248 | tf_op jit(solution)/shard_map/ppermute | solution.py:384
  15.2 3.1 %collective-permute-start.4 = (bf16[512,384]{1,0:T(8,128)(2,1)S(1)}, bf16[512,384]{1,0:T(8,128)(2,1)S(1)}, u32[]{:S(2)}, u32[]{:S(2)}) collective-permute-start(bf16[512,384]{1,0:T(8,128)(2,1)S(1)} %pair_up.3.got_ref), channel_id=1, source_target_pairs={{0,16},{8,120},{16,32},{24,8},{32,48},{40,24},{48,64},{56,40},{64,... | collective-permute-start | bytes 1179656 | tf_op jit(solution)/shard_map/ppermute | solution.py:384
  18.3 0.0 collective-permute-start.6
  18.3 1.6 %first_stats.1 = (f32[40,1024]{1,0:T(8,128)S(1)}, bf16[1024,384]{1,0:T(8,128)(2,1)S(1)}, f32[8,1024]{1,0:T(8,128)S(1)}) custom-call(bf16[512,384]{1,0:T(8,128)(2,1)S(1)} %pair_up.2.own_ref, bf16[512,384]{1,0:T(8,128)(2,1)S(1)} %pair_up.3.got_ref), custom_call_target="tpu_custom_call" | custom-call | flops 536870912 | bytes 2097152 | tf_op jit(solution)/shard_map/first_stats/pallas_call | solution.py:170
  20.0 3.1 %collective-permute-done.4.key.refs_7_ = bf16[512,384]{1,0:T(8,128)(2,1)S(1)} collective-permute-done((bf16[512,384]{1,0:T(8,128)(2,1)S(1)}, bf16[512,384]{1,0:T(8,128)(2,1)S(1)}, u32[]{:S(2)}, u32[]{:S(2)}) %collective-permute-start.4) | collective-permute-done | bytes 393248 | tf_op jit(solution)/shard_map/ppermute | solution.py:384
  23.0 3.1 %collective-permute-start.5 = (bf16[512,384]{1,0:T(8,128)(2,1)S(1)}, bf16[512,384]{1,0:T(8,128)(2,1)S(1)}, u32[]{:S(2)}, u32[]{:S(2)}) collective-permute-start(bf16[512,384]{1,0:T(8,128)(2,1)S(1)} %collective-permute-done.4.key.refs_7_), channel_id=1, source_target_pairs={{0,16},{8,120},{16,32},{24,8},{32,48},{40,24},{48,64},{56,40},{64,... | collective-permute-start | bytes 1179656 | tf_op jit(solution)/shard_map/ppermute | solution.py:384
  26.1 1.6 %more_stats.8.before = f32[40,1024]{1,0:T(8,128)S(1)} custom-call(bf16[1024,384]{1,0:T(8,128)(2,1)S(1)} %get-tuple-element.30.held, bf16[512,384]{1,0:T(8,128)(2,1)S(1)} %collective-permute-done.3.key.refs_6_, f32[40,1024]{1,0:T(8,128)S(1)} %get-tuple-element.35.before), custom_call_target="tpu_custom_call", output_to_operand_aliasing={{}: (2, {})} | custom-call | flops 536870912 | bytes 2097152 | tf_op jit(solution)/shard_map/more_stats/pallas_call | solution.py:187
  27.7 0.0 collective-permute-done.6.key.refs_0_
  27.7 2.6 %collective-permute-start.8 = (bf16[512,384]{1,0:T(8,128)(2,1)S(1)}, bf16[512,384]{1,0:T(8,128)(2,1)S(1)}, u32[]{:S(2)}, u32[]{:S(2)}) collective-permute-start(bf16[512,384]{1,0:T(8,128)(2,1)S(1)} %collective-permute-done.6.key.refs_0_), channel_id=1, source_target_pairs={{0,16},{8,120},{16,32},{24,8},{32,48},{40,24},{48,64},{56,40},{64,... | collective-permute-start | bytes 1179656 | tf_op jit(solution)/shard_map/ppermute | solution.py:384
  30.3 1.6 %more_stats.9.before = f32[40,1024]{1,0:T(8,128)S(1)} custom-call(bf16[1024,384]{1,0:T(8,128)(2,1)S(1)} %get-tuple-element.30.held, bf16[512,384]{1,0:T(8,128)(2,1)S(1)} %collective-permute-done.4.key.refs_7_, f32[40,1024]{1,0:T(8,128)S(1)} %more_stats.8.before), custom_call_target="tpu_custom_call", output_to_operand_aliasing={{}: (2, {})} | custom-call | flops 536870912 | bytes 2097152 | tf_op jit(solution)/shard_map/more_stats/pallas_call | solution.py:187
  31.9 0.0 collective-permute-done.5.key.refs_1_
  32.0 2.6 %collective-permute-start.7 = (bf16[512,384]{1,0:T(8,128)(2,1)S(1)}, bf16[512,384]{1,0:T(8,128)(2,1)S(1)}, u32[]{:S(2)}, u32[]{:S(2)}) collective-permute-start(bf16[512,384]{1,0:T(8,128)(2,1)S(1)} %collective-permute-done.5.key.refs_1_), channel_id=1, source_target_pairs={{0,16},{8,120},{16,32},{24,8},{32,48},{40,24},{48,64},{56,40},{64,... | collective-permute-start | bytes 1179656 | tf_op jit(solution)/shard_map/ppermute | solution.py:384
  34.5 1.6 %more_stats.10.before = f32[40,1024]{1,0:T(8,128)S(1)} custom-call(bf16[1024,384]{1,0:T(8,128)(2,1)S(1)} %get-tuple-element.30.held, bf16[512,384]{1,0:T(8,128)(2,1)S(1)} %collective-permute-done.6.key.refs_0_, f32[40,1024]{1,0:T(8,128)S(1)} %more_stats.9.before), custom_call_target="tpu_custom_call", output_to_operand_aliasing={{}: (2, {})} | custom-call | flops 536870912 | bytes 2097152 | tf_op jit(solution)/shard_map/more_stats/pallas_call | solution.py:187
  36.2 0.0 collective-permute-done.8.key.refs_2_
  36.2 2.7 %collective-permute-start.10 = (bf16[256,384]{1,0:T(8,128)(2,1)S(1)}, bf16[256,384]{1,0:T(8,128)(2,1)S(1)}, u32[]{:S(2)}, u32[]{:S(2)}) collective-permute-start(bf16[256,384]{1,0:T(8,128)(2,1)S(1)} %slice.10), channel_id=1, source_target_pairs={{0,16},{8,120},{16,32},{24,8},{32,48},{40,24},{48,64},{56,40},{64,... | collective-permute-start | bytes 589832 | tf_op jit(solution)/shard_map/ppermute | solution.py:384
  38.9 1.6 %more_stats.11.before = f32[40,1024]{1,0:T(8,128)S(1)} custom-call(bf16[1024,384]{1,0:T(8,128)(2,1)S(1)} %get-tuple-element.30.held, bf16[512,384]{1,0:T(8,128)(2,1)S(1)} %collective-permute-done.5.key.refs_1_, f32[40,1024]{1,0:T(8,128)S(1)} %more_stats.10.before), custom_call_target="tpu_custom_call", output_to_operand_aliasing={{}: (2, {})} | custom-call | flops 536870912 | bytes 2097152 | tf_op jit(solution)/shard_map/more_stats/pallas_call | solution.py:187
  40.5 0.0 collective-permute-done.7.key.refs_3_
  40.5 2.6 %collective-permute-start.9 = (bf16[256,384]{1,0:T(8,128)(2,1)S(1)}, bf16[256,384]{1,0:T(8,128)(2,1)S(1)}, u32[]{:S(2)}, u32[]{:S(2)}) collective-permute-start(bf16[256,384]{1,0:T(8,128)(2,1)S(1)} %slice.9), channel_id=1, source_target_pairs={{0,16},{8,120},{16,32},{24,8},{32,48},{40,24},{48,64},{56,40},{64,... | collective-permute-start | bytes 589832 | tf_op jit(solution)/shard_map/ppermute | solution.py:384
  43.1 1.6 %more_stats.12.before = f32[40,1024]{1,0:T(8,128)S(1)} custom-call(bf16[1024,384]{1,0:T(8,128)(2,1)S(1)} %get-tuple-element.30.held, bf16[512,384]{1,0:T(8,128)(2,1)S(1)} %collective-permute-done.8.key.refs_2_, f32[40,1024]{1,0:T(8,128)S(1)} %more_stats.11.before), custom_call_target="tpu_custom_call", output_to_operand_aliasing={{}: (2, {})} | custom-call | flops 536870912 | bytes 2097152 | tf_op jit(solution)/shard_map/more_stats/pallas_call | solution.py:187
  44.7 1.6 %more_stats.13.before = f32[40,1024]{1,0:T(8,128)S(1)} custom-call(bf16[1024,384]{1,0:T(8,128)(2,1)S(1)} %get-tuple-element.30.held, bf16[512,384]{1,0:T(8,128)(2,1)S(1)} %collective-permute-done.7.key.refs_3_, f32[40,1024]{1,0:T(8,128)S(1)} %more_stats.12.before), custom_call_target="tpu_custom_call", output_to_operand_aliasing={{}: (2, {})} | custom-call | flops 536870912 | bytes 2097152 | tf_op jit(solution)/shard_map/more_stats/pallas_call | solution.py:187
  46.3 0.0 collective-permute-done.10.key.refs_4_
  46.3 0.9 %more_stats.14.before = f32[40,1024]{1,0:T(8,128)S(1)} custom-call(bf16[1024,384]{1,0:T(8,128)(2,1)S(1)} %get-tuple-element.30.held, bf16[256,384]{1,0:T(8,128)(2,1)S(1)} %collective-permute-done.10.key.refs_4_, f32[40,1024]{1,0:T(8,128)S(1)} %more_stats.13.before), custom_call_target="tpu_custom_call", output_to_operand_aliasing={{}: (2, {})} | custom-call | flops 268435456 | bytes 1048576 | tf_op jit(solution)/shard_map/more_stats/pallas_call | solution.py:187
  47.2 1.0 %more_stats.15.mine = f32[8,1024]{1,0:T(8,128)S(1)} custom-call(bf16[1024,384]{1,0:T(8,128)(2,1)S(1)} %get-tuple-element.30.held, bf16[256,384]{1,0:T(8,128)(2,1)S(1)} %collective-permute-done.9.key.refs_5_, f32[40,1024]{1,0:T(8,128)S(1)} %more_stats.14.before), custom_call_target="tpu_custom_call" | custom-call | flops 268435456 | bytes 1048576 | tf_op jit(solution)/shard_map/more_stats/pallas_call | solution.py:187
  48.2 3.6 %collective-permute-start.11 = (f32[8,1024]{1,0:T(8,128)S(1)}, f32[8,1024]{1,0:T(8,128)S(1)}, u32[]{:S(2)}, u32[]{:S(2)}) collective-permute-start(f32[8,1024]{1,0:T(8,128)S(1)} %more_stats.15.mine), channel_id=1, source_target_pairs={{0,8},{8,0},{1,9},{9,1},{2,10},{10,2},{3,11},{11,3},{4,12},{12,4},... | collective-permute-start | bytes 98312 | tf_op jit(solution)/shard_map/ppermute | solution.py:393
  51.8 0.1 pad_add_fusion.place_ref
  51.9 0.8 collective-permute-done.11.sib
  52.7 0.8 merge.1
  53.5 5.6 %all-to-all-start = ((f32[8,2,1152]{2,1,0:T(2,128)}), f32[8,2,1152]{2,1,0:T(2,128)S(1)}, u32[]{:S(2)}, u32[]{:S(2)}) async-start(f32[8,2,1152]{2,1,0:T(2,128)} %get-tuple-element.45), calls=%async_computation | async-start | bytes 147456 | tf_op jit(solution)/shard_map/all_to_all | solution.py:426
  59.0 9.0 %row_part.1.refs_8_ = f32[1024,128]{1,0:T(8,128)} custom-call(bf16[1024,384]{1,0:T(8,128)(2,1)S(1)} %get-tuple-element.30.held, f32[8,1024]{1,0:T(8,128)S(1)} %get-tuple-element.46.norm_ref, bf16[512,384]{1,0:T(8,128)(2,1)S(1)} %collective-permute-done.6.key.refs_0_, bf16[512,384]{1,0:T(8,128)(2,1)S(1)} %copy-done.3, ...), custom_call_target="tpu_custom_call" | custom-call | flops 5368709120 | bytes 16777216 | tf_op jit(solution)/shard_map/row_part/pallas_call | solution.py:319
  68.1 5.2 %col_part.2 = (f32[112,256]{1,0:T(8,128)S(1)}, f32[112,256]{1,0:T(8,128)S(1)}, f32[16,1,128]{2,1,0:T(1,128)}) custom-call(s32[2]{0:T(128)S(1)} %pad_add_fusion.place_ref, bf16[1024,384]{1,0:T(8,128)(2,1)S(1)} %get-tuple-element.30.held, f32[8,2,1152]{2,1,0:T(2,128)S(1)} %all-to-all-done.stat_ref, bf16[512,384]{1,0:T(8,128)(2,1)S(1)} %collective-permute-done.6.key.refs_0_, ...), custom_call_target="tpu_custom_call" | custom-call | flops 2684354560 | bytes 8388608 | tf_op jit(solution)/shard_map/col_part/pallas_call | solution.py:370
  73.3 1.2 %collective-permute-start.12 = (f32[112,256]{1,0:T(8,128)S(1)}, f32[112,256]{1,0:T(8,128)S(1)}, u32[]{:S(2)}, u32[]{:S(2)}) collective-permute-start(f32[112,256]{1,0:T(8,128)S(1)} %get-tuple-element.48), channel_id=1, source_target_pairs={{0,128},{128,0},{1,129},{129,1},{2,130},{130,2},{3,131},{131,3},{4... | collective-permute-start | bytes 344072 | tf_op jit(solution)/shard_map/ppermute | solution.py:393
  74.4 1.2 %collective-permute-start.13 = (f32[112,256]{1,0:T(8,128)S(1)}, f32[112,256]{1,0:T(8,128)S(1)}, u32[]{:S(2)}, u32[]{:S(2)}) collective-permute-start(f32[112,256]{1,0:T(8,128)S(1)} %get-tuple-element.49), channel_id=1, source_target_pairs={{0,136},{8,128},{128,8},{136,0},{1,137},{9,129},{129,9},{137,1},{2... | collective-permute-start | bytes 344072 | tf_op jit(solution)/shard_map/ppermute | solution.py:393
  75.6 6.5 %all-to-all-start.1 = ((f32[16,1,128]{2,1,0:T(1,128)}), f32[16,1,128]{2,1,0:T(1,128)S(1)}, u32[]{:S(2)}, u32[]{:S(2)}) async-start(f32[16,1,128]{2,1,0:T(1,128)} %get-tuple-element.47), calls=%async_computation.1 | async-start | bytes 16384 | tf_op jit(solution)/shard_map/all_to_all | solution.py:430
  82.2 0.0 collective-permute-done.12
  82.2 0.0 collective-permute-done.13
  82.2 5.5 %col_part.3 = (f32[112,256]{1,0:T(8,128)S(1)}, f32[112,256]{1,0:T(8,128)S(1)}) custom-call(s32[2]{0:T(128)S(1)} %pad_add_fusion.place_ref, bf16[1024,384]{1,0:T(8,128)(2,1)S(1)} %get-tuple-element.30.held, f32[8,2,1152]{2,1,0:T(2,128)S(1)} %all-to-all-done.stat_ref, bf16[512,384]{1,0:T(8,128)(2,1)S(1)} %collective-permute-done.6.key.refs_0_, ...), custom_call_target="tpu_custom_call" | custom-call | flops 2684354560 | bytes 8388608 | tf_op jit(solution)/shard_map/col_part/pallas_call | solution.py:370
  87.7 0.1 collective-permute-start.14
  87.8 0.7 all-to-all-done.1
  88.5 0.6 slice_reduce_fusion
  89.8 0.7 fusion
  (17 shorter events, 0.2 us)
Async XLA Ops:
  1.8 4.4 %collective-permute-start = (bf16[256,384]{1,0:T(8,128)(2,1)S(1)}, bf16[256,384]{1,0:T(8,128)(2,1)S(1)}, u32[]{:S(2)}, u32[]{:S(2)}) collective-permute-start(bf16[256,384]{1,0:T(8,128)(2,1)S(1)} %get-tuple-element.28.own), channel_id=1, source_target_pairs={{0,8},{8,0},{1,9},{9,1},{2,10},{10,2},{3,11},{11,3},{4,12},{12,4},... | collective-permute-start | bytes 589832 | tf_op jit(solution)/shard_map/ppermute | solution.py:393
  5.2 6.5 %collective-permute-start.1 = (bf16[256,384]{1,0:T(8,128)(2,1)S(1)}, bf16[256,384]{1,0:T(8,128)(2,1)S(1)}, u32[]{:S(2)}, u32[]{:S(2)}) collective-permute-start(bf16[256,384]{1,0:T(8,128)(2,1)S(1)} %get-tuple-element.29), channel_id=1, source_target_pairs={{0,128},{128,0},{1,129},{129,1},{2,130},{130,2},{3,131},{131,3},{4... | collective-permute-start | bytes 589832 | tf_op jit(solution)/shard_map/ppermute | solution.py:393
  6.3 8.9 %collective-permute-start.3 = (bf16[512,384]{1,0:T(8,128)(2,1)S(1)}, bf16[512,384]{1,0:T(8,128)(2,1)S(1)}, u32[]{:S(2)}, u32[]{:S(2)}) collective-permute-start(bf16[512,384]{1,0:T(8,128)(2,1)S(1)} %pair_up.2.own_ref), channel_id=1, source_target_pairs={{0,16},{8,120},{16,32},{24,8},{32,48},{40,24},{48,64},{56,40},{64,... | collective-permute-start | bytes 1179656 | tf_op jit(solution)/shard_map/ppermute | solution.py:384
  11.6 1.9 %collective-permute-start.2 = (bf16[256,384]{1,0:T(8,128)(2,1)S(1)}, bf16[256,384]{1,0:T(8,128)(2,1)S(1)}, u32[]{:S(2)}, u32[]{:S(2)}) collective-permute-start(bf16[256,384]{1,0:T(8,128)(2,1)S(1)} %collective-permute-done.1.own), channel_id=1, source_target_pairs={{0,8},{8,0},{1,9},{9,1},{2,10},{10,2},{3,11},{11,3},{4,12},{12,4},... | collective-permute-start | bytes 589832 | tf_op jit(solution)/shard_map/ppermute | solution.py:393
  15.2 11.0 %copy-start = (bf16[512,384]{1,0:T(8,128)(2,1)}, bf16[512,384]{1,0:T(8,128)(2,1)S(1)}, u32[]{:S(2)}) copy-start(bf16[512,384]{1,0:T(8,128)(2,1)S(1)} %collective-permute-done.3.key.refs_6_) | copy-start | bytes 1179652
  15.2 7.8 %collective-permute-start.4 = (bf16[512,384]{1,0:T(8,128)(2,1)S(1)}, bf16[512,384]{1,0:T(8,128)(2,1)S(1)}, u32[]{:S(2)}, u32[]{:S(2)}) collective-permute-start(bf16[512,384]{1,0:T(8,128)(2,1)S(1)} %pair_up.3.got_ref), channel_id=1, source_target_pairs={{0,16},{8,120},{16,32},{24,8},{32,48},{40,24},{48,64},{56,40},{64,... | collective-permute-start | bytes 1179656 | tf_op jit(solution)/shard_map/ppermute | solution.py:384
  18.3 9.4 %collective-permute-start.6 = (bf16[512,384]{1,0:T(8,128)(2,1)S(1)}, bf16[512,384]{1,0:T(8,128)(2,1)S(1)}, u32[]{:S(2)}, u32[]{:S(2)}) collective-permute-start(bf16[512,384]{1,0:T(8,128)(2,1)S(1)} %collective-permute-done.3.key.refs_6_), channel_id=1, source_target_pairs={{0,16},{8,120},{16,32},{24,8},{32,48},{40,24},{48,64},{56,40},{64,... | collective-permute-start | bytes 1179656 | tf_op jit(solution)/shard_map/ppermute | solution.py:384
  23.0 7.3 %copy-start.1 = (bf16[512,384]{1,0:T(8,128)(2,1)}, bf16[512,384]{1,0:T(8,128)(2,1)S(1)}, u32[]{:S(2)}) copy-start(bf16[512,384]{1,0:T(8,128)(2,1)S(1)} %collective-permute-done.4.key.refs_7_) | copy-start | bytes 1179652
  23.0 8.9 %collective-permute-start.5 = (bf16[512,384]{1,0:T(8,128)(2,1)S(1)}, bf16[512,384]{1,0:T(8,128)(2,1)S(1)}, u32[]{:S(2)}, u32[]{:S(2)}) collective-permute-start(bf16[512,384]{1,0:T(8,128)(2,1)S(1)} %collective-permute-done.4.key.refs_7_), channel_id=1, source_target_pairs={{0,16},{8,120},{16,32},{24,8},{32,48},{40,24},{48,64},{56,40},{64,... | collective-permute-start | bytes 1179656 | tf_op jit(solution)/shard_map/ppermute | solution.py:384
  27.7 8.4 %collective-permute-start.8 = (bf16[512,384]{1,0:T(8,128)(2,1)S(1)}, bf16[512,384]{1,0:T(8,128)(2,1)S(1)}, u32[]{:S(2)}, u32[]{:S(2)}) collective-permute-start(bf16[512,384]{1,0:T(8,128)(2,1)S(1)} %collective-permute-done.6.key.refs_0_), channel_id=1, source_target_pairs={{0,16},{8,120},{16,32},{24,8},{32,48},{40,24},{48,64},{56,40},{64,... | collective-permute-start | bytes 1179656 | tf_op jit(solution)/shard_map/ppermute | solution.py:384
  31.9 6.9 %copy-start.2 = (bf16[512,384]{1,0:T(8,128)(2,1)}, bf16[512,384]{1,0:T(8,128)(2,1)S(1)}, u32[]{:S(2)}) copy-start(bf16[512,384]{1,0:T(8,128)(2,1)S(1)} %collective-permute-done.5.key.refs_1_) | copy-start | bytes 1179652
  32.0 8.5 %collective-permute-start.7 = (bf16[512,384]{1,0:T(8,128)(2,1)S(1)}, bf16[512,384]{1,0:T(8,128)(2,1)S(1)}, u32[]{:S(2)}, u32[]{:S(2)}) collective-permute-start(bf16[512,384]{1,0:T(8,128)(2,1)S(1)} %collective-permute-done.5.key.refs_1_), channel_id=1, source_target_pairs={{0,16},{8,120},{16,32},{24,8},{32,48},{40,24},{48,64},{56,40},{64,... | collective-permute-start | bytes 1179656 | tf_op jit(solution)/shard_map/ppermute | solution.py:384
  36.2 10.1 %collective-permute-start.10 = (bf16[256,384]{1,0:T(8,128)(2,1)S(1)}, bf16[256,384]{1,0:T(8,128)(2,1)S(1)}, u32[]{:S(2)}, u32[]{:S(2)}) collective-permute-start(bf16[256,384]{1,0:T(8,128)(2,1)S(1)} %slice.10), channel_id=1, source_target_pairs={{0,16},{8,120},{16,32},{24,8},{32,48},{40,24},{48,64},{56,40},{64,... | collective-permute-start | bytes 589832 | tf_op jit(solution)/shard_map/ppermute | solution.py:384
  40.5 6.7 %collective-permute-start.9 = (bf16[256,384]{1,0:T(8,128)(2,1)S(1)}, bf16[256,384]{1,0:T(8,128)(2,1)S(1)}, u32[]{:S(2)}, u32[]{:S(2)}) collective-permute-start(bf16[256,384]{1,0:T(8,128)(2,1)S(1)} %slice.9), channel_id=1, source_target_pairs={{0,16},{8,120},{16,32},{24,8},{32,48},{40,24},{48,64},{56,40},{64,... | collective-permute-start | bytes 589832 | tf_op jit(solution)/shard_map/ppermute | solution.py:384
  47.2 11.8 %copy-start.3 = (bf16[512,384]{1,0:T(8,128)(2,1)S(1)}, bf16[512,384]{1,0:T(8,128)(2,1)}, u32[]{:S(2)}) copy-start(bf16[512,384]{1,0:T(8,128)(2,1)} %copy-done.2) | copy-start | bytes 1179652
  48.2 4.5 %collective-permute-start.11 = (f32[8,1024]{1,0:T(8,128)S(1)}, f32[8,1024]{1,0:T(8,128)S(1)}, u32[]{:S(2)}, u32[]{:S(2)}) collective-permute-start(f32[8,1024]{1,0:T(8,128)S(1)} %more_stats.15.mine), channel_id=1, source_target_pairs={{0,8},{8,0},{1,9},{9,1},{2,10},{10,2},{3,11},{11,3},{4,12},{12,4},... | collective-permute-start | bytes 98312 | tf_op jit(solution)/shard_map/ppermute | solution.py:393
  53.5 14.6 %all-to-all-start = ((f32[8,2,1152]{2,1,0:T(2,128)}), f32[8,2,1152]{2,1,0:T(2,128)S(1)}, u32[]{:S(2)}, u32[]{:S(2)}) async-start(f32[8,2,1152]{2,1,0:T(2,128)} %get-tuple-element.45), calls=%async_computation | async-start | bytes 147456 | tf_op jit(solution)/shard_map/all_to_all | solution.py:426
  73.3 8.9 %collective-permute-start.12 = (f32[112,256]{1,0:T(8,128)S(1)}, f32[112,256]{1,0:T(8,128)S(1)}, u32[]{:S(2)}, u32[]{:S(2)}) collective-permute-start(f32[112,256]{1,0:T(8,128)S(1)} %get-tuple-element.48), channel_id=1, source_target_pairs={{0,128},{128,0},{1,129},{129,1},{2,130},{130,2},{3,131},{131,3},{4... | collective-permute-start | bytes 344072 | tf_op jit(solution)/shard_map/ppermute | solution.py:393
  74.4 7.7 %collective-permute-start.13 = (f32[112,256]{1,0:T(8,128)S(1)}, f32[112,256]{1,0:T(8,128)S(1)}, u32[]{:S(2)}, u32[]{:S(2)}) collective-permute-start(f32[112,256]{1,0:T(8,128)S(1)} %get-tuple-element.49), channel_id=1, source_target_pairs={{0,136},{8,128},{128,8},{136,0},{1,137},{9,129},{129,9},{137,1},{2... | collective-permute-start | bytes 344072 | tf_op jit(solution)/shard_map/ppermute | solution.py:393
  75.6 12.9 %all-to-all-start.1 = ((f32[16,1,128]{2,1,0:T(1,128)}), f32[16,1,128]{2,1,0:T(1,128)S(1)}, u32[]{:S(2)}, u32[]{:S(2)}) async-start(f32[16,1,128]{2,1,0:T(1,128)} %get-tuple-element.47), calls=%async_computation.1 | async-start | bytes 16384 | tf_op jit(solution)/shard_map/all_to_all | solution.py:430
  87.7 2.1 %collective-permute-start.14 = (f32[112,256]{1,0:T(8,128)S(1)}, f32[112,256]{1,0:T(8,128)S(1)}, u32[]{:S(2)}, u32[]{:S(2)}) collective-permute-start(f32[112,256]{1,0:T(8,128)S(1)} %get-tuple-element.52), channel_id=1, source_target_pairs={{0,8},{8,0},{1,9},{9,1},{2,10},{10,2},{3,11},{11,3},{4,12},{12,4},... | collective-permute-start | bytes 344072 | tf_op jit(solution)/shard_map/ppermute | solution.py:393
where the time goes:
time: 91.9 us; the launch traced here: 91.6 us
  starting transfers between devices  43.3 us (47%)
  Pallas kernels  34.8 us (38%)
  waiting for transfers between devices  9.43 us (10%)
  between operations  2.63 us (3%)
  other arithmetic  1.43 us (2%)
    ppermute x8, starting transfers between devices, onward(): return lax.ppermute(array, ('z', 'c'), pairs)  20.9 us
    pallas_call x8, Pallas kernels, more_stats(): pl.pallas_call(functools.partial(more_kernel, last), out_shape=jax.ShapeD...  11.5 us
    pallas_call x2, Pallas kernels, col_part(): pl.pallas_call(functools.partial(col_kernel, query_at), out_shape=(part,...  10.7 us
    ppermute x7, starting transfers between devices, swap(): return lax.ppermute(array, axis, [(i, n - 1 - i) for i in range(n)])  10.3 us
    pallas_call x1, Pallas kernels, row_part(): pl.pallas_call(row_kernel, out_shape=pltpu.HBM((4 * TOK, 128), F32), in_s...  9 us
    all_to_all x1, starting transfers between devices, local(): losses = lax.all_to_all(loss, ('yl', *HEAD), 0, 0, tiled=True)  6.52 us
    all_to_all x1, starting transfers between devices, local(): stats = lax.all_to_all(send, 'z', 0, 0, tiled=True)  5.56 us
    ppermute x8, waiting for transfers between devices, onward(): return lax.ppermute(array, ('z', 'c'), pairs)  4.62 us
  transfers between devices with their start and end apart: 17, of which 7 were waited for; matrix products, arithmetic and copies ran while one was open for 1% of the time, Pallas kernels for 29%

commit v1 on v0

--- a/solution.py
+++ b/solution.py
@@ -244,7 +244,7 @@
 class Keys:
     def __init__(self, held, refs, late, sems):
         self.held, self.near, self.opposite, self.far, self.late = held, refs[:4], refs[4:6], refs[6:8], late
-        self.copies = [pltpu.make_async_copy(self.far[i], late.at[i], sems.at[i]) for i in range(2)]
+        self.copies = [pltpu.make_async_copy(self.far[0], late.at[0], sems.at[0])]
 
     def start(self):
         for copy in self.copies:
@@ -261,7 +261,7 @@
             return self.near[slot - 1][:, columns]
         if slot == 5:
             return jnp.concatenate([self.opposite[0][:, columns], self.opposite[1][:, columns]], axis=0)
-        return self.late[slot - 6, :, columns]
+        return self.late[0, :, columns] if slot == 6 else self.far[1][:, columns]
 
     def piece(self, i, columns):
         if i < 4:
@@ -270,16 +270,16 @@
             return self.held[(i - 4) * 2 * TOK : (i - 4) * 2 * TOK + TOK, columns]
         if i < 8:
             return self.opposite[i - 6][:, columns]
-        return self.late[i - 8, :, columns]
+        return self.late[0, :, columns] if i == 8 else self.far[1][:, columns]
 
 
 STEPS = (0, 2, 2, 3, 3, 4, 1, 1)
-KEY_SPECS = whole(6) + [HBM] * 2
-KEY_SCRATCH = [pltpu.VMEM((2, 2 * TOK, PACK), BF16), pltpu.SemaphoreType.DMA((4,))]
+KEY_SPECS = whole(6) + [HBM] + whole(1)
+KEY_SCRATCH = [pltpu.VMEM((1, 2 * TOK, PACK), BF16), pltpu.SemaphoreType.DMA((4,))]
 
 
 def as_operands(packets):
-    return [*packets[:6], *(in_hbm(p) for p in packets[6:])]
+    return [*packets[:6], in_hbm(packets[6]), packets[7]]
 
 
 def row_kernel(held, norm_ref, *refs):

time: 91.9 us -> 95.1 us (1.035)
  other arithmetic: 1.43 us -> 3.03 us
  local copies, waits for them, and re-layouts: 0.06 us -> 1.61 us
    add x1, other arithmetic: 0.02 us -> 1.61 us  [local(): other = swap(far_keep, 'yl') + swap(far_give, ('yl', 'c'))]
  transfers between devices with their start and end apart: 17 -> 17, of which waited for: 7 -> 6; matrix products, arithmetic and copies ran while one was open for 1% -> 3% of each run, Pallas kernels for 29% -> 28%
where the time goes in v1:
time: 95.1 us; the launch traced here: 94.7 us
  starting transfers between devices  43.4 us (46%)
  Pallas kernels  35.3 us (37%)
  waiting for transfers between devices  8.77 us (9%)
  other arithmetic  3.03 us (3%)
  between operations  2.61 us (3%)
  local copies, waits for them, and re-layouts  1.61 us (2%)
    ppermute x8, starting transfers between devices, onward(): return lax.ppermute(array, ('z', 'c'), pairs)  20.8 us
    pallas_call x8, Pallas kernels, more_stats(): pl.pallas_call(functools.partial(more_kernel, last), out_shape=jax.ShapeD...  11.5 us
    pallas_call x2, Pallas kernels, col_part(): pl.pallas_call(functools.partial(col_kernel, query_at), out_shape=(part,...  11.2 us
    ppermute x7, starting transfers between devices, swap(): return lax.ppermute(array, axis, [(i, n - 1 - i) for i in range(n)])  10.5 us
    pallas_call x1, Pallas kernels, row_part(): pl.pallas_call(row_kernel, out_shape=pltpu.HBM((4 * TOK, 128), F32), in_s...  9.02 us
    all_to_all x1, starting transfers between devices, local(): losses = lax.all_to_all(loss, ('yl', *HEAD), 0, 0, tiled=True)  6.52 us
    all_to_all x1, starting transfers between devices, local(): stats = lax.all_to_all(send, 'z', 0, 0, tiled=True)  5.56 us
    ppermute x8, waiting for transfers between devices, onward(): return lax.ppermute(array, ('z', 'c'), pairs)  4.62 us
  transfers between devices with their start and end apart: 17, of which 6 were waited for; matrix products, arithmetic and copies ran while one was open for 3% of the time, Pallas kernels for 28%

profile of v1, /device:TPU:1, one launch (start us, length us, event | category | flops | bytes accessed | tf_op | source)
XLA Modules:
  0.0 94.7 jit_solution(11769462578338851422)
XLA Ops:
  0.6 1.2 %prepare.1 = (bf16[256,384]{1,0:T(8,128)(2,1)S(1)}, bf16[256,384]{1,0:T(8,128)(2,1)S(1)}) custom-call(s32[1]{0:T(128)} %bitcast.2.yl_ref, bf16[256,512]{1,0:T(8,128)(2,1)} %bitcast.12, bf16[224,256]{1,0:T(8,128)(2,1)} %bitcast.13, f32[1,256]{1,0:T(1,128)} %bitcast.14), custom_call_target="tpu_custom_call" | custom-call | tf_op jit(solution)/shard_map/prepare/pallas_call | solution.py:75
  1.8 3.3 %collective-permute-start = (bf16[256,384]{1,0:T(8,128)(2,1)S(1)}, bf16[256,384]{1,0:T(8,128)(2,1)S(1)}, u32[]{:S(2)}, u32[]{:S(2)}) collective-permute-start(bf16[256,384]{1,0:T(8,128)(2,1)S(1)} %get-tuple-element.28.own), channel_id=1, source_target_pairs={{0,8},{8,0},{1,9},{9,1},{2,10},{10,2},{3,11},{11,3},{4,12},{12,4},... | collective-permute-start | bytes 589832 | tf_op jit(solution)/shard_map/ppermute | solution.py:393
  5.2 0.0 collective-permute-start.1
  5.2 1.1 %collective-permute-done.sib = bf16[256,384]{1,0:T(8,128)(2,1)S(1)} collective-permute-done((bf16[256,384]{1,0:T(8,128)(2,1)S(1)}, bf16[256,384]{1,0:T(8,128)(2,1)S(1)}, u32[]{:S(2)}, u32[]{:S(2)}) %collective-permute-start) | collective-permute-done | bytes 196640 | tf_op jit(solution)/shard_map/ppermute | solution.py:393
  6.3 4.2 %collective-permute-start.3 = (bf16[512,384]{1,0:T(8,128)(2,1)S(1)}, bf16[512,384]{1,0:T(8,128)(2,1)S(1)}, u32[]{:S(2)}, u32[]{:S(2)}) collective-permute-start(bf16[512,384]{1,0:T(8,128)(2,1)S(1)} %pair_up.2.own_ref), channel_id=1, source_target_pairs={{0,16},{8,120},{16,32},{24,8},{32,48},{40,24},{48,64},{56,40},{64,... | collective-permute-start | bytes 1179656 | tf_op jit(solution)/shard_map/ppermute | solution.py:384
  10.4 1.2 %collective-permute-done.1.own = bf16[256,384]{1,0:T(8,128)(2,1)S(1)} collective-permute-done((bf16[256,384]{1,0:T(8,128)(2,1)S(1)}, bf16[256,384]{1,0:T(8,128)(2,1)S(1)}, u32[]{:S(2)}, u32[]{:S(2)}) %collective-permute-start.1) | collective-permute-done | bytes 196640 | tf_op jit(solution)/shard_map/ppermute | solution.py:393
  11.6 0.9 collective-permute-start.2
  12.5 1.1 %collective-permute-done.2.sib = bf16[256,384]{1,0:T(8,128)(2,1)S(1)} collective-permute-done((bf16[256,384]{1,0:T(8,128)(2,1)S(1)}, bf16[256,384]{1,0:T(8,128)(2,1)S(1)}, u32[]{:S(2)}, u32[]{:S(2)}) %collective-permute-start.2) | collective-permute-done | bytes 196640 | tf_op jit(solution)/shard_map/ppermute | solution.py:393
  13.6 1.6 %collective-permute-done.3.key.refs_6_ = bf16[512,384]{1,0:T(8,128)(2,1)S(1)} collective-permute-done((bf16[512,384]{1,0:T(8,128)(2,1)S(1)}, bf16[512,384]{1,0:T(8,128)(2,1)S(1)}, u32[]{:S(2)}, u32[]{:S(2)}) %collective-permute-start.3) | collective-permute-done | bytes 393248 | tf_op jit(solution)/shard_map/ppermute | solution.py:384
  15.2 3.1 %collective-permute-start.4 = (bf16[512,384]{1,0:T(8,128)(2,1)S(1)}, bf16[512,384]{1,0:T(8,128)(2,1)S(1)}, u32[]{:S(2)}, u32[]{:S(2)}) collective-permute-start(bf16[512,384]{1,0:T(8,128)(2,1)S(1)} %pair_up.3.got_ref), channel_id=1, source_target_pairs={{0,16},{8,120},{16,32},{24,8},{32,48},{40,24},{48,64},{56,40},{64,... | collective-permute-start | bytes 1179656 | tf_op jit(solution)/shard_map/ppermute | solution.py:384
  18.3 0.0 collective-permute-start.6
  18.3 1.6 %first_stats.1 = (f32[40,1024]{1,0:T(8,128)S(1)}, bf16[1024,384]{1,0:T(8,128)(2,1)S(1)}, f32[8,1024]{1,0:T(8,128)S(1)}) custom-call(bf16[512,384]{1,0:T(8,128)(2,1)S(1)} %pair_up.2.own_ref, bf16[512,384]{1,0:T(8,128)(2,1)S(1)} %pair_up.3.got_ref), custom_call_target="tpu_custom_call" | custom-call | flops 536870912 | bytes 2097152 | tf_op jit(solution)/shard_map/first_stats/pallas_call | solution.py:170
  20.0 3.1 %collective-permute-done.4.key.refs_7_ = bf16[512,384]{1,0:T(8,128)(2,1)S(1)} collective-permute-done((bf16[512,384]{1,0:T(8,128)(2,1)S(1)}, bf16[512,384]{1,0:T(8,128)(2,1)S(1)}, u32[]{:S(2)}, u32[]{:S(2)}) %collective-permute-start.4) | collective-permute-done | bytes 393248 | tf_op jit(solution)/shard_map/ppermute | solution.py:384
  23.0 3.1 %collective-permute-start.5 = (bf16[512,384]{1,0:T(8,128)(2,1)S(1)}, bf16[512,384]{1,0:T(8,128)(2,1)S(1)}, u32[]{:S(2)}, u32[]{:S(2)}) collective-permute-start(bf16[512,384]{1,0:T(8,128)(2,1)S(1)} %collective-permute-done.4.key.refs_7_), channel_id=1, source_target_pairs={{0,16},{8,120},{16,32},{24,8},{32,48},{40,24},{48,64},{56,40},{64,... | collective-permute-start | bytes 1179656 | tf_op jit(solution)/shard_map/ppermute | solution.py:384
  26.1 1.6 %more_stats.8.before = f32[40,1024]{1,0:T(8,128)S(1)} custom-call(bf16[1024,384]{1,0:T(8,128)(2,1)S(1)} %get-tuple-element.30.held, bf16[512,384]{1,0:T(8,128)(2,1)S(1)} %collective-permute-done.3.key.refs_6_, f32[40,1024]{1,0:T(8,128)S(1)} %get-tuple-element.35.before), custom_call_target="tpu_custom_call", output_to_operand_aliasing={{}: (2, {})} | custom-call | flops 536870912 | bytes 2097152 | tf_op jit(solution)/shard_map/more_stats/pallas_call | solution.py:187
  27.7 2.6 %collective-permute-start.8 = (bf16[512,384]{1,0:T(8,128)(2,1)S(1)}, bf16[512,384]{1,0:T(8,128)(2,1)S(1)}, u32[]{:S(2)}, u32[]{:S(2)}) collective-permute-start(bf16[512,384]{1,0:T(8,128)(2,1)S(1)} %collective-permute-done.6.key.refs_0_), channel_id=1, source_target_pairs={{0,16},{8,120},{16,32},{24,8},{32,48},{40,24},{48,64},{56,40},{64,... | collective-permute-start | bytes 1179656 | tf_op jit(solution)/shard_map/ppermute | solution.py:384
  30.3 1.6 %more_stats.9.before = f32[40,1024]{1,0:T(8,128)S(1)} custom-call(bf16[1024,384]{1,0:T(8,128)(2,1)S(1)} %get-tuple-element.30.held, bf16[512,384]{1,0:T(8,128)(2,1)S(1)} %collective-permute-done.4.key.refs_7_, f32[40,1024]{1,0:T(8,128)S(1)} %more_stats.8.before), custom_call_target="tpu_custom_call", output_to_operand_aliasing={{}: (2, {})} | custom-call | flops 536870912 | bytes 2097152 | tf_op jit(solution)/shard_map/more_stats/pallas_call | solution.py:187
  31.9 0.0 collective-permute-done.5.key.refs_1_
  32.0 2.6 %collective-permute-start.7 = (bf16[512,384]{1,0:T(8,128)(2,1)S(1)}, bf16[512,384]{1,0:T(8,128)(2,1)S(1)}, u32[]{:S(2)}, u32[]{:S(2)}) collective-permute-start(bf16[512,384]{1,0:T(8,128)(2,1)S(1)} %collective-permute-done.5.key.refs_1_), channel_id=1, source_target_pairs={{0,16},{8,120},{16,32},{24,8},{32,48},{40,24},{48,64},{56,40},{64,... | collective-permute-start | bytes 1179656 | tf_op jit(solution)/shard_map/ppermute | solution.py:384
  34.5 1.6 %more_stats.10.before = f32[40,1024]{1,0:T(8,128)S(1)} custom-call(bf16[1024,384]{1,0:T(8,128)(2,1)S(1)} %get-tuple-element.30.held, bf16[512,384]{1,0:T(8,128)(2,1)S(1)} %collective-permute-done.6.key.refs_0_, f32[40,1024]{1,0:T(8,128)S(1)} %more_stats.9.before), custom_call_target="tpu_custom_call", output_to_operand_aliasing={{}: (2, {})} | custom-call | flops 536870912 | bytes 2097152 | tf_op jit(solution)/shard_map/more_stats/pallas_call | solution.py:187
  36.2 0.0 collective-permute-done.8.key.refs_2_
  36.2 2.7 %collective-permute-start.10 = (bf16[256,384]{1,0:T(8,128)(2,1)S(1)}, bf16[256,384]{1,0:T(8,128)(2,1)S(1)}, u32[]{:S(2)}, u32[]{:S(2)}) collective-permute-start(bf16[256,384]{1,0:T(8,128)(2,1)S(1)} %slice.10), channel_id=1, source_target_pairs={{0,16},{8,120},{16,32},{24,8},{32,48},{40,24},{48,64},{56,40},{64,... | collective-permute-start | bytes 589832 | tf_op jit(solution)/shard_map/ppermute | solution.py:384
  38.9 1.6 %more_stats.11.before = f32[40,1024]{1,0:T(8,128)S(1)} custom-call(bf16[1024,384]{1,0:T(8,128)(2,1)S(1)} %get-tuple-element.30.held, bf16[512,384]{1,0:T(8,128)(2,1)S(1)} %collective-permute-done.5.key.refs_1_, f32[40,1024]{1,0:T(8,128)S(1)} %more_stats.10.before), custom_call_target="tpu_custom_call", output_to_operand_aliasing={{}: (2, {})} | custom-call | flops 536870912 | bytes 2097152 | tf_op jit(solution)/shard_map/more_stats/pallas_call | solution.py:187
  40.5 0.7 slice.9
  41.2 2.5 %collective-permute-start.9 = (bf16[256,384]{1,0:T(8,128)(2,1)}, bf16[256,384]{1,0:T(8,128)(2,1)S(1)}, u32[]{:S(2)}, u32[]{:S(2)}) collective-permute-start(bf16[256,384]{1,0:T(8,128)(2,1)} %slice.9), channel_id=1, source_target_pairs={{0,16},{8,120},{16,32},{24,8},{32,48},{40,24},{48,64},{56,40},{64,... | collective-permute-start | bytes 589832 | tf_op jit(solution)/shard_map/ppermute | solution.py:384
  43.7 1.6 %more_stats.12.before = f32[40,1024]{1,0:T(8,128)S(1)} custom-call(bf16[1024,384]{1,0:T(8,128)(2,1)S(1)} %get-tuple-element.30.held, bf16[512,384]{1,0:T(8,128)(2,1)S(1)} %collective-permute-done.8.key.refs_2_, f32[40,1024]{1,0:T(8,128)S(1)} %more_stats.11.before), custom_call_target="tpu_custom_call", output_to_operand_aliasing={{}: (2, {})} | custom-call | flops 536870912 | bytes 2097152 | tf_op jit(solution)/shard_map/more_stats/pallas_call | solution.py:187
  45.3 1.6 %more_stats.13.before = f32[40,1024]{1,0:T(8,128)S(1)} custom-call(bf16[1024,384]{1,0:T(8,128)(2,1)S(1)} %get-tuple-element.30.held, bf16[512,384]{1,0:T(8,128)(2,1)S(1)} %collective-permute-done.7.key.refs_3_, f32[40,1024]{1,0:T(8,128)S(1)} %more_stats.12.before), custom_call_target="tpu_custom_call", output_to_operand_aliasing={{}: (2, {})} | custom-call | flops 536870912 | bytes 2097152 | tf_op jit(solution)/shard_map/more_stats/pallas_call | solution.py:187
  46.9 0.0 collective-permute-done.10.key.refs_4_
  46.9 0.9 more_stats.14.before
  47.8 1.0 %more_stats.15.mine = f32[8,1024]{1,0:T(8,128)S(1)} custom-call(bf16[1024,384]{1,0:T(8,128)(2,1)S(1)} %get-tuple-element.30.held, bf16[256,384]{1,0:T(8,128)(2,1)S(1)} %collective-permute-done.9.key.refs_5_, f32[40,1024]{1,0:T(8,128)S(1)} %more_stats.14.before), custom_call_target="tpu_custom_call" | custom-call | flops 268435456 | bytes 1048576 | tf_op jit(solution)/shard_map/more_stats/pallas_call | solution.py:187
  48.8 3.9 %collective-permute-start.11 = (f32[8,1024]{1,0:T(8,128)S(1)}, f32[8,1024]{1,0:T(8,128)S(1)}, u32[]{:S(2)}, u32[]{:S(2)}) collective-permute-start(f32[8,1024]{1,0:T(8,128)S(1)} %more_stats.15.mine), channel_id=1, source_target_pairs={{0,8},{8,0},{1,9},{9,1},{2,10},{10,2},{3,11},{11,3},{4,12},{12,4},... | collective-permute-start | bytes 98312 | tf_op jit(solution)/shard_map/ppermute | solution.py:393
  52.7 0.1 pad_add_fusion.place_ref
  52.7 0.8 collective-permute-done.11.sib
  53.5 0.8 merge.1
  54.3 5.6 %all-to-all-start = ((f32[8,2,1152]{2,1,0:T(2,128)}), f32[8,2,1152]{2,1,0:T(2,128)S(1)}, u32[]{:S(2)}, u32[]{:S(2)}) async-start(f32[8,2,1152]{2,1,0:T(2,128)} %get-tuple-element.45), calls=%async_computation | async-start | bytes 147456 | tf_op jit(solution)/shard_map/all_to_all | solution.py:426
  59.8 9.0 %row_part.1.refs_8_ = f32[1024,128]{1,0:T(8,128)} custom-call(bf16[1024,384]{1,0:T(8,128)(2,1)S(1)} %get-tuple-element.30.held, f32[8,1024]{1,0:T(8,128)S(1)} %get-tuple-element.46.norm_ref, bf16[512,384]{1,0:T(8,128)(2,1)S(1)} %collective-permute-done.6.key.refs_0_, bf16[512,384]{1,0:T(8,128)(2,1)S(1)} %copy-done.2, ...), custom_call_target="tpu_custom_call" | custom-call | flops 5368709120 | bytes 16777216 | tf_op jit(solution)/shard_map/row_part/pallas_call | solution.py:319
  68.9 5.8 %col_part.2 = (f32[112,256]{1,0:T(8,128)S(1)}, f32[112,256]{1,0:T(8,128)S(1)}, f32[16,1,128]{2,1,0:T(1,128)}) custom-call(s32[2]{0:T(128)S(1)} %pad_add_fusion.place_ref, bf16[1024,384]{1,0:T(8,128)(2,1)S(1)} %get-tuple-element.30.held, f32[8,2,1152]{2,1,0:T(2,128)S(1)} %all-to-all-done.stat_ref, bf16[512,384]{1,0:T(8,128)(2,1)S(1)} %collective-permute-done.6.key.refs_0_, ...), custom_call_target="tpu_custom_call" | custom-call | flops 2684354560 | bytes 8388608 | tf_op jit(solution)/shard_map/col_part/pallas_call | solution.py:370
  74.7 1.1 %collective-permute-start.12 = (f32[112,256]{1,0:T(8,128)S(1)}, f32[112,256]{1,0:T(8,128)}, u32[]{:S(2)}, u32[]{:S(2)}) collective-permute-start(f32[112,256]{1,0:T(8,128)S(1)} %get-tuple-element.48), channel_id=1, source_target_pairs={{0,128},{128,0},{1,129},{129,1},{2,130},{130,2},{3,131},{131,3},{4... | collective-permute-start | bytes 344072 | tf_op jit(solution)/shard_map/ppermute | solution.py:393
  75.8 1.2 %collective-permute-start.13 = (f32[112,256]{1,0:T(8,128)S(1)}, f32[112,256]{1,0:T(8,128)}, u32[]{:S(2)}, u32[]{:S(2)}) collective-permute-start(f32[112,256]{1,0:T(8,128)S(1)} %get-tuple-element.49), channel_id=1, source_target_pairs={{0,136},{8,128},{128,8},{136,0},{1,137},{9,129},{129,9},{137,1},{2... | collective-permute-start | bytes 344072 | tf_op jit(solution)/shard_map/ppermute | solution.py:393
  77.0 6.5 %all-to-all-start.1 = ((f32[16,1,128]{2,1,0:T(1,128)}), f32[16,1,128]{2,1,0:T(1,128)S(1)}, u32[]{:S(2)}, u32[]{:S(2)}) async-start(f32[16,1,128]{2,1,0:T(1,128)} %get-tuple-element.47), calls=%async_computation.1 | async-start | bytes 16384 | tf_op jit(solution)/shard_map/all_to_all | solution.py:430
  83.6 0.0 collective-permute-done.13
  83.6 1.6 %add.6 = f32[112,256]{1,0:T(8,128)} add(f32[112,256]{1,0:T(8,128)} %collective-permute-done.12, f32[112,256]{1,0:T(8,128)} %collective-permute-done.13) | non-fusion elementwise | flops 28672 | bytes 344064 | tf_op jit(solution)/shard_map/add | solution.py:431
  85.2 5.4 %col_part.3 = (f32[112,256]{1,0:T(8,128)S(1)}, f32[112,256]{1,0:T(8,128)S(1)}) custom-call(s32[2]{0:T(128)S(1)} %pad_add_fusion.place_ref, bf16[1024,384]{1,0:T(8,128)(2,1)S(1)} %get-tuple-element.30.held, f32[8,2,1152]{2,1,0:T(2,128)S(1)} %all-to-all-done.stat_ref, bf16[512,384]{1,0:T(8,128)(2,1)S(1)} %collective-permute-done.6.key.refs_0_, ...), custom_call_target="tpu_custom_call" | custom-call | flops 2684354560 | bytes 8388608 | tf_op jit(solution)/shard_map/col_part/pallas_call | solution.py:370
  90.6 0.1 collective-permute-start.14
  90.7 0.6 slice_reduce_fusion
  92.0 0.0 collective-permute-done.14
  92.0 0.9 copy-done.3
  92.9 0.7 fusion
  (17 shorter events, 0.1 us)
Async XLA Ops:
  1.8 4.4 %collective-permute-start = (bf16[256,384]{1,0:T(8,128)(2,1)S(1)}, bf16[256,384]{1,0:T(8,128)(2,1)S(1)}, u32[]{:S(2)}, u32[]{:S(2)}) collective-permute-start(bf16[256,384]{1,0:T(8,128)(2,1)S(1)} %get-tuple-element.28.own), channel_id=1, source_target_pairs={{0,8},{8,0},{1,9},{9,1},{2,10},{10,2},{3,11},{11,3},{4,12},{12,4},... | collective-permute-start | bytes 589832 | tf_op jit(solution)/shard_map/ppermute | solution.py:393
  5.2 6.5 %collective-permute-start.1 = (bf16[256,384]{1,0:T(8,128)(2,1)S(1)}, bf16[256,384]{1,0:T(8,128)(2,1)S(1)}, u32[]{:S(2)}, u32[]{:S(2)}) collective-permute-start(bf16[256,384]{1,0:T(8,128)(2,1)S(1)} %get-tuple-element.29), channel_id=1, source_target_pairs={{0,128},{128,0},{1,129},{129,1},{2,130},{130,2},{3,131},{131,3},{4... | collective-permute-start | bytes 589832 | tf_op jit(solution)/shard_map/ppermute | solution.py:393
  6.3 8.9 %collective-permute-start.3 = (bf16[512,384]{1,0:T(8,128)(2,1)S(1)}, bf16[512,384]{1,0:T(8,128)(2,1)S(1)}, u32[]{:S(2)}, u32[]{:S(2)}) collective-permute-start(bf16[512,384]{1,0:T(8,128)(2,1)S(1)} %pair_up.2.own_ref), channel_id=1, source_target_pairs={{0,16},{8,120},{16,32},{24,8},{32,48},{40,24},{48,64},{56,40},{64,... | collective-permute-start | bytes 1179656 | tf_op jit(solution)/shard_map/ppermute | solution.py:384
  11.6 1.9 %collective-permute-start.2 = (bf16[256,384]{1,0:T(8,128)(2,1)S(1)}, bf16[256,384]{1,0:T(8,128)(2,1)S(1)}, u32[]{:S(2)}, u32[]{:S(2)}) collective-permute-start(bf16[256,384]{1,0:T(8,128)(2,1)S(1)} %collective-permute-done.1.own), channel_id=1, source_target_pairs={{0,8},{8,0},{1,9},{9,1},{2,10},{10,2},{3,11},{11,3},{4,12},{12,4},... | collective-permute-start | bytes 589832 | tf_op jit(solution)/shard_map/ppermute | solution.py:393
  15.2 11.0 %copy-start = (bf16[512,384]{1,0:T(8,128)(2,1)}, bf16[512,384]{1,0:T(8,128)(2,1)S(1)}, u32[]{:S(2)}) copy-start(bf16[512,384]{1,0:T(8,128)(2,1)S(1)} %collective-permute-done.3.key.refs_6_) | copy-start | bytes 1179652
  15.2 7.8 %collective-permute-start.4 = (bf16[512,384]{1,0:T(8,128)(2,1)S(1)}, bf16[512,384]{1,0:T(8,128)(2,1)S(1)}, u32[]{:S(2)}, u32[]{:S(2)}) collective-permute-start(bf16[512,384]{1,0:T(8,128)(2,1)S(1)} %pair_up.3.got_ref), channel_id=1, source_target_pairs={{0,16},{8,120},{16,32},{24,8},{32,48},{40,24},{48,64},{56,40},{64,... | collective-permute-start | bytes 1179656 | tf_op jit(solution)/shard_map/ppermute | solution.py:384
  18.3 9.4 %collective-permute-start.6 = (bf16[512,384]{1,0:T(8,128)(2,1)S(1)}, bf16[512,384]{1,0:T(8,128)(2,1)S(1)}, u32[]{:S(2)}, u32[]{:S(2)}) collective-permute-start(bf16[512,384]{1,0:T(8,128)(2,1)S(1)} %collective-permute-done.3.key.refs_6_), channel_id=1, source_target_pairs={{0,16},{8,120},{16,32},{24,8},{32,48},{40,24},{48,64},{56,40},{64,... | collective-permute-start | bytes 1179656 | tf_op jit(solution)/shard_map/ppermute | solution.py:384
  23.0 8.9 %collective-permute-start.5 = (bf16[512,384]{1,0:T(8,128)(2,1)S(1)}, bf16[512,384]{1,0:T(8,128)(2,1)S(1)}, u32[]{:S(2)}, u32[]{:S(2)}) collective-permute-start(bf16[512,384]{1,0:T(8,128)(2,1)S(1)} %collective-permute-done.4.key.refs_7_), channel_id=1, source_target_pairs={{0,16},{8,120},{16,32},{24,8},{32,48},{40,24},{48,64},{56,40},{64,... | collective-permute-start | bytes 1179656 | tf_op jit(solution)/shard_map/ppermute | solution.py:384
  27.7 8.4 %collective-permute-start.8 = (bf16[512,384]{1,0:T(8,128)(2,1)S(1)}, bf16[512,384]{1,0:T(8,128)(2,1)S(1)}, u32[]{:S(2)}, u32[]{:S(2)}) collective-permute-start(bf16[512,384]{1,0:T(8,128)(2,1)S(1)} %collective-permute-done.6.key.refs_0_), channel_id=1, source_target_pairs={{0,16},{8,120},{16,32},{24,8},{32,48},{40,24},{48,64},{56,40},{64,... | collective-permute-start | bytes 1179656 | tf_op jit(solution)/shard_map/ppermute | solution.py:384
  31.9 6.9 %copy-start.1 = (bf16[512,384]{1,0:T(8,128)(2,1)}, bf16[512,384]{1,0:T(8,128)(2,1)S(1)}, u32[]{:S(2)}) copy-start(bf16[512,384]{1,0:T(8,128)(2,1)S(1)} %collective-permute-done.5.key.refs_1_) | copy-start | bytes 1179652
  32.0 8.5 %collective-permute-start.7 = (bf16[512,384]{1,0:T(8,128)(2,1)S(1)}, bf16[512,384]{1,0:T(8,128)(2,1)S(1)}, u32[]{:S(2)}, u32[]{:S(2)}) collective-permute-start(bf16[512,384]{1,0:T(8,128)(2,1)S(1)} %collective-permute-done.5.key.refs_1_), channel_id=1, source_target_pairs={{0,16},{8,120},{16,32},{24,8},{32,48},{40,24},{48,64},{56,40},{64,... | collective-permute-start | bytes 1179656 | tf_op jit(solution)/shard_map/ppermute | solution.py:384
  36.2 10.7 %collective-permute-start.10 = (bf16[256,384]{1,0:T(8,128)(2,1)S(1)}, bf16[256,384]{1,0:T(8,128)(2,1)S(1)}, u32[]{:S(2)}, u32[]{:S(2)}) collective-permute-start(bf16[256,384]{1,0:T(8,128)(2,1)S(1)} %slice.10), channel_id=1, source_target_pairs={{0,16},{8,120},{16,32},{24,8},{32,48},{40,24},{48,64},{56,40},{64,... | collective-permute-start | bytes 589832 | tf_op jit(solution)/shard_map/ppermute | solution.py:384
  41.2 6.7 %collective-permute-start.9 = (bf16[256,384]{1,0:T(8,128)(2,1)}, bf16[256,384]{1,0:T(8,128)(2,1)S(1)}, u32[]{:S(2)}, u32[]{:S(2)}) collective-permute-start(bf16[256,384]{1,0:T(8,128)(2,1)} %slice.9), channel_id=1, source_target_pairs={{0,16},{8,120},{16,32},{24,8},{32,48},{40,24},{48,64},{56,40},{64,... | collective-permute-start | bytes 589832 | tf_op jit(solution)/shard_map/ppermute | solution.py:384
  47.8 12.0 %copy-start.2 = (bf16[512,384]{1,0:T(8,128)(2,1)S(1)}, bf16[512,384]{1,0:T(8,128)(2,1)}, u32[]{:S(2)}) copy-start(bf16[512,384]{1,0:T(8,128)(2,1)} %copy-done.1) | copy-start | bytes 1179652
  48.8 4.7 %collective-permute-start.11 = (f32[8,1024]{1,0:T(8,128)S(1)}, f32[8,1024]{1,0:T(8,128)S(1)}, u32[]{:S(2)}, u32[]{:S(2)}) collective-permute-start(f32[8,1024]{1,0:T(8,128)S(1)} %more_stats.15.mine), channel_id=1, source_target_pairs={{0,8},{8,0},{1,9},{9,1},{2,10},{10,2},{3,11},{11,3},{4,12},{12,4},... | collective-permute-start | bytes 98312 | tf_op jit(solution)/shard_map/ppermute | solution.py:393
  54.3 14.6 %all-to-all-start = ((f32[8,2,1152]{2,1,0:T(2,128)}), f32[8,2,1152]{2,1,0:T(2,128)S(1)}, u32[]{:S(2)}, u32[]{:S(2)}) async-start(f32[8,2,1152]{2,1,0:T(2,128)} %get-tuple-element.45), calls=%async_computation | async-start | bytes 147456 | tf_op jit(solution)/shard_map/all_to_all | solution.py:426
  74.7 8.9 %collective-permute-start.12 = (f32[112,256]{1,0:T(8,128)S(1)}, f32[112,256]{1,0:T(8,128)}, u32[]{:S(2)}, u32[]{:S(2)}) collective-permute-start(f32[112,256]{1,0:T(8,128)S(1)} %get-tuple-element.48), channel_id=1, source_target_pairs={{0,128},{128,0},{1,129},{129,1},{2,130},{130,2},{3,131},{131,3},{4... | collective-permute-start | bytes 344072 | tf_op jit(solution)/shard_map/ppermute | solution.py:393
  75.8 7.7 %collective-permute-start.13 = (f32[112,256]{1,0:T(8,128)S(1)}, f32[112,256]{1,0:T(8,128)}, u32[]{:S(2)}, u32[]{:S(2)}) collective-permute-start(f32[112,256]{1,0:T(8,128)S(1)} %get-tuple-element.49), channel_id=1, source_target_pairs={{0,136},{8,128},{128,8},{136,0},{1,137},{9,129},{129,9},{137,1},{2... | collective-permute-start | bytes 344072 | tf_op jit(solution)/shard_map/ppermute | solution.py:393
  77.0 13.6 %all-to-all-start.1 = ((f32[16,1,128]{2,1,0:T(1,128)}), f32[16,1,128]{2,1,0:T(1,128)S(1)}, u32[]{:S(2)}, u32[]{:S(2)}) async-start(f32[16,1,128]{2,1,0:T(1,128)} %get-tuple-element.47), calls=%async_computation.1 | async-start | bytes 16384 | tf_op jit(solution)/shard_map/all_to_all | solution.py:430
  90.6 1.4 %collective-permute-start.14 = (f32[112,256]{1,0:T(8,128)S(1)}, f32[112,256]{1,0:T(8,128)S(1)}, u32[]{:S(2)}, u32[]{:S(2)}) collective-permute-start(f32[112,256]{1,0:T(8,128)S(1)} %get-tuple-element.52), channel_id=1, source_target_pairs={{0,8},{8,0},{1,9},{9,1},{2,10},{10,2},{3,11},{11,3},{4,12},{12,4},... | collective-permute-start | bytes 344072 | tf_op jit(solution)/shard_map/ppermute | solution.py:393
  92.0 0.9 copy-start.3
